TPU v7x, 256 devices: a whole 4x4x8 slice. The times are simulated.
256 devices in a mesh: row: 16 (over z, core), col: 16 (over x, y).
Axes of the slice: x: 4, y: 4, z: 8, core: 2. Of those that a mesh axis runs over, the one named last changes fastest.
Arguments:
- front_values: float32 [2, 16, 512, 2, 16, 512], P(None, 'row', None, None, 'col'), as said below
- block_pattern: int32 [32, 32], replicated, may hold values from 0 to 1, as said below
- panel_order: int32 [32], replicated, may hold values from 0 to 31, each once
Outputs:
- factor: float32 [2, 16, 512, 2, 16, 512], P(None, 'row', None, None, 'col')
Inputs may be any that keep to these rules, and one draw needn't show every extreme that they name: front_values is symmetric, and with block_pattern applied it is positive definite. `block_pattern`: symmetric, with ones on the diagonal. `panel_order`: each of 0 to 31 once; the first 3 entries are the block columns eliminated, in order.
All inputs are finite; a program needn't handle non-finite values.
Results may differ from a plain program's by a relative error of at most 0.0001.
Values sent between devices are 32-bit elements; how exact they have to be, the bound alone decides.
A program may use at most 128 MiB of HBM per device.

v0:
```python
import jax
import jax.numpy as jnp
from jax import lax
from jax.sharding import PartitionSpec as P

PANELS = 3


precise = lax.Precision.HIGHEST


def broadcast(block, axis, holder):
    block = jnp.where(lax.axis_index(axis) == holder, block, jnp.zeros_like(block))
    return lax.psum(block, axis)


def product(first, second):
    return jnp.dot(first, second, precision=precise, preferred_element_type=jnp.float32)


def diagonal_slot(matrix_now, pivot_block, row_count, col_count):
    row_slab = lax.dynamic_index_in_dim(matrix_now, pivot_block // row_count, 0, keepdims=False)
    return lax.dynamic_index_in_dim(row_slab, pivot_block // col_count, 1, keepdims=False)


def factor_share(diag_block, pivot_block, row_count, col_count):
    owner = (lax.axis_index("row") == pivot_block % row_count) & (
        lax.axis_index("col") == pivot_block % col_count
    )
    identity = jnp.eye(diag_block.shape[0], dtype=jnp.float32)
    safe_block = jnp.where(owner, diag_block, identity)
    lower_factor = jnp.linalg.cholesky(safe_block)
    inverse = jax.scipy.linalg.solve_triangular(lower_factor, identity, lower=True)
    inverse = broadcast(inverse, "col", pivot_block % col_count)
    inverse = broadcast(inverse, "row", pivot_block % row_count)
    return (lower_factor, inverse)


def eliminate(matrix_now, finished, pivot_block, lower_factor, inverse):
    row_count = lax.axis_size("row")
    col_count = lax.axis_size("col")
    row_here = lax.axis_index("row")
    col_here = lax.axis_index("col")
    row_blocks = matrix_now.shape[0]
    block_width = matrix_now.shape[1]
    col_blocks = matrix_now.shape[2]
    row_ids = jnp.arange(row_blocks, dtype=jnp.int32) * row_count + row_here
    col_ids = jnp.arange(col_blocks, dtype=jnp.int32) * col_count + col_here
    row_done = lax.dynamic_index_in_dim(
        finished.reshape(row_blocks, row_count), row_here, 1, keepdims=False
    )
    col_done = lax.dynamic_index_in_dim(
        finished.reshape(col_blocks, col_count), col_here, 1, keepdims=False
    )
    row_left = 1.0 - row_done - (row_ids == pivot_block).astype(jnp.float32)
    col_left = 1.0 - col_done - (col_ids == pivot_block).astype(jnp.float32)
    row_slot = pivot_block // row_count
    col_slot = pivot_block // col_count
    column_raw = lax.dynamic_index_in_dim(matrix_now, col_slot, 2, keepdims=False).reshape(
        row_blocks * block_width, block_width
    )
    row_raw = lax.dynamic_index_in_dim(matrix_now, row_slot, 0, keepdims=False).reshape(
        block_width, col_blocks * block_width
    )
    column_panel = broadcast(product(column_raw, inverse.T), "col", pivot_block % col_count)
    row_panel = broadcast(product(inverse, row_raw), "row", pivot_block % row_count)
    left_factor = column_panel * jnp.repeat(row_left, block_width)[:, None]
    right_factor = row_panel * jnp.repeat(col_left, block_width)[None, :]
    updated = matrix_now - product(left_factor, right_factor).reshape(matrix_now.shape)
    col_owner = col_here == pivot_block % col_count
    row_owner = row_here == pivot_block % row_count
    old_column = lax.dynamic_index_in_dim(updated, col_slot, 2, keepdims=False)
    new_column = jnp.where(
        col_owner & (row_left[:, None, None] > 0),
        column_panel.reshape(row_blocks, block_width, block_width),
        old_column,
    )
    updated = lax.dynamic_update_index_in_dim(updated, new_column, col_slot, 2)
    old_row = lax.dynamic_index_in_dim(updated, row_slot, 0, keepdims=False)
    new_row = jnp.where(
        row_owner & (col_left[None, :, None] > 0),
        row_panel.reshape(block_width, col_blocks, block_width),
        old_row,
    )
    old_diag = lax.dynamic_index_in_dim(new_row, col_slot, 1, keepdims=False)
    new_diag = jnp.where(row_owner & col_owner, lower_factor, old_diag)
    new_row = lax.dynamic_update_index_in_dim(new_row, new_diag, col_slot, 1)
    updated = lax.dynamic_update_index_in_dim(updated, new_row, row_slot, 0)
    total_blocks = finished.shape[0]
    finished = finished + (jnp.arange(total_blocks, dtype=jnp.int32) == pivot_block).astype(
        jnp.float32
    )
    return (updated, finished, left_factor, right_factor)


def per_device(front_values, block_pattern, panel_order):
    row_count = lax.axis_size("row")
    col_count = lax.axis_size("col")
    row_here = lax.axis_index("row")
    col_here = lax.axis_index("col")
    row_blocks = front_values.shape[0]
    block_width = front_values.shape[2]
    col_blocks = front_values.shape[3]
    matrix_now = front_values.reshape(row_blocks, block_width, col_blocks, block_width)
    local_pattern = block_pattern.reshape(row_blocks, row_count, col_blocks, col_count)
    local_pattern = lax.dynamic_index_in_dim(local_pattern, row_here, 1, keepdims=False)
    local_pattern = lax.dynamic_index_in_dim(local_pattern, col_here, 2, keepdims=False)
    matrix_now = matrix_now * local_pattern.astype(jnp.float32)[:, None, :, None]
    finished = jnp.zeros((row_blocks * row_count,), jnp.float32)

    def advance(section_index, carried):
        current, done_now = carried
        pivot_block = panel_order[section_index]
        diag_block = diagonal_slot(current, pivot_block, row_count, col_count)
        lower_now, inverse_now = factor_share(diag_block, pivot_block, row_count, col_count)
        result = eliminate(current, done_now, pivot_block, lower_now, inverse_now)
        return (result[0], result[1])

    matrix_now = lax.fori_loop(0, PANELS, advance, (matrix_now, finished))[0]
    return matrix_now.reshape(front_values.shape)


def solution(mesh):
    return jax.shard_map(
        per_device,
        mesh=mesh,
        in_specs=(P(None, "row", None, None, "col", None), P(), P()),
        out_specs=P(None, "row", None, None, "col", None),
        check_vma=False,
    )
```

profile of v0, /device:TPU:1, one launch (start us, length us, event | category | flops | bytes accessed | tf_op | source)
XLA Modules:
  0.0 1931.9 jit_solution(3155844212053122032)
XLA Ops:
  12.7 1903.6 %while.23 = (s32[]{:T(128)}, f32[2,512,2,512]{3,1,0,2:T(8,128)}, f32[32]{0:T(128)S(1)}, s32[32]{0:T(128)S(1)}, s32[]{:T(128)}, /*index=5*/s32[]{:T(128)}, s32[]{...) while((s32[]{:T(128)}, f32[2,512,2,512]{3,1,0,2:T(8,128)}, ...), condition=%wide.region_13.14_spmd.clone, body=%wide.region_0.13_spmd.clone.sunk | while | flops 14307622912 | bytes 233413008 | solution.py:119
  18.4 11.7 cholesky.522
  30.2 9.8 custom-call.106
  40.7 11.7 cholesky.525
  52.8 10.3 custom-call.107
  65.1 11.7 cholesky.527
  76.9 9.8 custom-call.108
  88.4 11.9 cholesky.528
  106.3 11.9 while.24
  118.2 39.3 %custom-call.110 = f32[4,128,128]{1,2,0:T(8,128)S(1)} custom-call(f32[4,128,128]{2,1,0:T(8,128)S(1)} %get-tuple-element.303), custom_call_target="InvertDiagBlocksLowerTriangular" | custom-call | tf_op jit(solution)/shard_map/while/body/eval_jaxpr/jit(_solve_triangular)/triangular_solve | solution.py:33
  167.2 99.6 %all-reduce.6.cloned.1.call-done = f32[512,512]{0,1:T(8,128)} async-done(((f32[512,512]{0,1:T(8,128)}), f32[512,512]{0,1:T(8,128)}) %all-reduce.6.cloned.1.call-update) | async-done | bytes 1048592 | tf_op jit(solution)/shard_map/while/body/eval_jaxpr/psum | solution.py:14
  275.1 106.0 %all-reduce.8.cloned.1.call-done = f32[512,512]{0,1:T(8,128)} async-done(((f32[512,512]{0,1:T(8,128)}), f32[512,512]{0,1:T(8,128)}) %all-reduce.8.cloned.1.call-update) | async-done | bytes 1048592 | tf_op jit(solution)/shard_map/while/body/eval_jaxpr/psum | solution.py:14
  381.1 9.3 convolution_select_fusion.4
  399.5 105.9 %all-reduce.10.cloned.1.call-done = f32[512,1024]{1,0:T(8,128)} async-done(((f32[512,1024]{1,0:T(8,128)}), f32[512,1024]{1,0:T(8,128)}) %all-reduce.10.cloned.1.call-update) | async-done | bytes 2097168 | tf_op jit(solution)/shard_map/while/body/eval_jaxpr/psum | solution.py:14
  516.3 92.4 %all-reduce.12.cloned.1.call-done = f32[1024,512]{1,0:T(8,128)} async-done(((f32[1024,512]{1,0:T(8,128)}), f32[1024,512]{1,0:T(8,128)}) %all-reduce.12.cloned.1.call-update) | async-done | bytes 2097168 | tf_op jit(solution)/shard_map/while/body/eval_jaxpr/psum | solution.py:14
  608.7 9.7 fusion.134
  618.4 6.6 reshape.341
  654.0 11.7 cholesky.522
  665.8 9.8 custom-call.106
  676.2 11.7 cholesky.525
  688.3 10.0 custom-call.107
  700.3 11.7 cholesky.527
  712.2 9.8 custom-call.108
  723.7 12.1 cholesky.528
  741.7 11.9 while.24
  753.7 39.3 %custom-call.110 = f32[4,128,128]{1,2,0:T(8,128)S(1)} custom-call(f32[4,128,128]{2,1,0:T(8,128)S(1)} %get-tuple-element.303), custom_call_target="InvertDiagBlocksLowerTriangular" | custom-call | tf_op jit(solution)/shard_map/while/body/eval_jaxpr/jit(_solve_triangular)/triangular_solve | solution.py:33
  802.7 96.3 %all-reduce.6.cloned.1.call-done = f32[512,512]{0,1:T(8,128)} async-done(((f32[512,512]{0,1:T(8,128)}), f32[512,512]{0,1:T(8,128)}) %all-reduce.6.cloned.1.call-update) | async-done | bytes 1048592 | tf_op jit(solution)/shard_map/while/body/eval_jaxpr/psum | solution.py:14
  907.3 105.9 %all-reduce.8.cloned.1.call-done = f32[512,512]{0,1:T(8,128)} async-done(((f32[512,512]{0,1:T(8,128)}), f32[512,512]{0,1:T(8,128)}) %all-reduce.8.cloned.1.call-update) | async-done | bytes 1048592 | tf_op jit(solution)/shard_map/while/body/eval_jaxpr/psum | solution.py:14
  1013.2 9.3 convolution_select_fusion.4
  1031.6 105.9 %all-reduce.10.cloned.1.call-done = f32[512,1024]{1,0:T(8,128)} async-done(((f32[512,1024]{1,0:T(8,128)}), f32[512,1024]{1,0:T(8,128)}) %all-reduce.10.cloned.1.call-update) | async-done | bytes 2097168 | tf_op jit(solution)/shard_map/while/body/eval_jaxpr/psum | solution.py:14
  1148.1 92.8 %all-reduce.12.cloned.1.call-done = f32[1024,512]{1,0:T(8,128)} async-done(((f32[1024,512]{1,0:T(8,128)}), f32[1024,512]{1,0:T(8,128)}) %all-reduce.12.cloned.1.call-update) | async-done | bytes 2097168 | tf_op jit(solution)/shard_map/while/body/eval_jaxpr/psum | solution.py:14
  1240.9 9.7 fusion.134
  1286.5 11.7 cholesky.522
  1298.2 9.8 custom-call.106
  1308.7 11.7 cholesky.525
  1320.8 10.0 custom-call.107
  1332.8 11.7 cholesky.527
  1344.6 9.8 custom-call.108
  1356.1 11.9 cholesky.528
  1374.0 11.9 while.24
  1385.9 39.3 %custom-call.110 = f32[4,128,128]{1,2,0:T(8,128)S(1)} custom-call(f32[4,128,128]{2,1,0:T(8,128)S(1)} %get-tuple-element.303), custom_call_target="InvertDiagBlocksLowerTriangular" | custom-call | tf_op jit(solution)/shard_map/while/body/eval_jaxpr/jit(_solve_triangular)/triangular_solve | solution.py:33
  1434.9 96.3 %all-reduce.6.cloned.1.call-done = f32[512,512]{0,1:T(8,128)} async-done(((f32[512,512]{0,1:T(8,128)}), f32[512,512]{0,1:T(8,128)}) %all-reduce.6.cloned.1.call-update) | async-done | bytes 1048592 | tf_op jit(solution)/shard_map/while/body/eval_jaxpr/psum | solution.py:14
  1539.8 105.6 %all-reduce.8.cloned.1.call-done = f32[512,512]{0,1:T(8,128)} async-done(((f32[512,512]{0,1:T(8,128)}), f32[512,512]{0,1:T(8,128)}) %all-reduce.8.cloned.1.call-update) | async-done | bytes 1048592 | tf_op jit(solution)/shard_map/while/body/eval_jaxpr/psum | solution.py:14
  1645.4 9.3 convolution_select_fusion.4
  1663.8 105.9 %all-reduce.10.cloned.1.call-done = f32[512,1024]{1,0:T(8,128)} async-done(((f32[512,1024]{1,0:T(8,128)}), f32[512,1024]{1,0:T(8,128)}) %all-reduce.10.cloned.1.call-update) | async-done | bytes 2097168 | tf_op jit(solution)/shard_map/while/body/eval_jaxpr/psum | solution.py:14
  1780.3 92.7 %all-reduce.12.cloned.1.call-done = f32[1024,512]{1,0:T(8,128)} async-done(((f32[1024,512]{1,0:T(8,128)}), f32[1024,512]{1,0:T(8,128)}) %all-reduce.12.cloned.1.call-update) | async-done | bytes 2097168 | tf_op jit(solution)/shard_map/while/body/eval_jaxpr/psum | solution.py:14
  1873.0 9.7 fusion.134
  1916.3 8.5 copy.82
  (371 shorter events, 270.4 us)
Async XLA Ops:
  7.6 5.0 copy-start.8
  12.7 254.1 %all-reduce.6.cloned.1.call-start = ((), (), s32[]{:S(2)}) async-start(), calls=%async_computation | async-start | bytes 2097152 | tf_op jit(solution)/shard_map/while/body/eval_jaxpr/psum | solution.py:14
  18.4 34.4 %copy-start.6 = (f32[512,512]{1,0:T(8,128)}, f32[512,512]{1,0:T(8,128)S(1)}, u32[]{:S(2)}) copy-start(f32[512,512]{1,0:T(8,128)S(1)} %fusion.124) | copy-start | bytes 3145732 | tf_op jit(solution)/shard_map/while
  157.5 4.1 copy-start.7
  167.2 213.9 %all-reduce.8.cloned.1.call-start = ((), (), s32[]{:S(2)}) async-start(), calls=%async_computation.1 | async-start | bytes 2097152 | tf_op jit(solution)/shard_map/while/body/eval_jaxpr/psum | solution.py:14
  267.9 237.6 %all-reduce.10.cloned.1.call-start = ((), (), s32[]{:S(2)}) async-start(), calls=%async_computation.2 | async-start | bytes 4194304 | tf_op jit(solution)/shard_map/while/body/eval_jaxpr/psum | solution.py:14
  390.4 1.9 copy-start.5
  390.4 218.3 %all-reduce.12.cloned.1.call-start = ((), (), s32[]{:S(2)}) async-start(), calls=%async_computation.3 | async-start | bytes 4194304 | tf_op jit(solution)/shard_map/while/body/eval_jaxpr/psum | solution.py:14
  505.4 4.6 copy-start.1
  625.0 4.8 copy-start.2
  629.8 1.6 copy-start.3
  631.4 2.1 copy-start
  631.4 2.1 copy-start.4
  648.2 250.8 %all-reduce.6.cloned.1.call-start = ((), (), s32[]{:S(2)}) async-start(), calls=%async_computation | async-start | bytes 2097152 | tf_op jit(solution)/shard_map/while/body/eval_jaxpr/psum | solution.py:14
  654.0 34.4 %copy-start.6 = (f32[512,512]{1,0:T(8,128)}, f32[512,512]{1,0:T(8,128)S(1)}, u32[]{:S(2)}) copy-start(f32[512,512]{1,0:T(8,128)S(1)} %fusion.124) | copy-start | bytes 3145732 | tf_op jit(solution)/shard_map/while
  793.0 4.1 copy-start.7
  802.6 210.5 %all-reduce.8.cloned.1.call-start = ((), (), s32[]{:S(2)}) async-start(), calls=%async_computation.1 | async-start | bytes 2097152 | tf_op jit(solution)/shard_map/while/body/eval_jaxpr/psum | solution.py:14
  900.1 237.4 %all-reduce.10.cloned.1.call-start = ((), (), s32[]{:S(2)}) async-start(), calls=%async_computation.2 | async-start | bytes 4194304 | tf_op jit(solution)/shard_map/while/body/eval_jaxpr/psum | solution.py:14
  1022.4 1.9 copy-start.5
  1022.5 218.5 %all-reduce.12.cloned.1.call-start = ((), (), s32[]{:S(2)}) async-start(), calls=%async_computation.3 | async-start | bytes 4194304 | tf_op jit(solution)/shard_map/while/body/eval_jaxpr/psum | solution.py:14
  1137.5 4.3 copy-start.1
  1257.2 4.8 copy-start.2
  1262.1 1.6 copy-start.3
  1263.6 2.1 copy-start
  1263.6 2.1 copy-start.4
  1280.7 250.6 %all-reduce.6.cloned.1.call-start = ((), (), s32[]{:S(2)}) async-start(), calls=%async_computation | async-start | bytes 2097152 | tf_op jit(solution)/shard_map/while/body/eval_jaxpr/psum | solution.py:14
  1286.4 34.3 %copy-start.6 = (f32[512,512]{1,0:T(8,128)}, f32[512,512]{1,0:T(8,128)S(1)}, u32[]{:S(2)}) copy-start(f32[512,512]{1,0:T(8,128)S(1)} %fusion.124) | copy-start | bytes 3145732 | tf_op jit(solution)/shard_map/while
  1425.2 4.1 copy-start.7
  1434.9 210.5 %all-reduce.8.cloned.1.call-start = ((), (), s32[]{:S(2)}) async-start(), calls=%async_computation.1 | async-start | bytes 2097152 | tf_op jit(solution)/shard_map/while/body/eval_jaxpr/psum | solution.py:14
  1532.3 237.4 %all-reduce.10.cloned.1.call-start = ((), (), s32[]{:S(2)}) async-start(), calls=%async_computation.2 | async-start | bytes 4194304 | tf_op jit(solution)/shard_map/while/body/eval_jaxpr/psum | solution.py:14
  1654.7 1.9 copy-start.5
  1654.7 218.3 %all-reduce.12.cloned.1.call-start = ((), (), s32[]{:S(2)}) async-start(), calls=%async_computation.3 | async-start | bytes 4194304 | tf_op jit(solution)/shard_map/while/body/eval_jaxpr/psum | solution.py:14
  1769.7 4.3 copy-start.1
  1889.3 4.8 copy-start.2
  1894.1 1.6 copy-start.3
  1895.7 2.1 copy-start
  1895.7 2.1 copy-start.4
Sparse Core Ops, SparseCore 0:
  167.3 99.4 all-reduce.5
  269.1 111.9 all-reduce.7
  390.5 114.8 all-reduce.9
  508.9 99.7 all-reduce.11
  802.8 96.1 all-reduce.5
  901.2 111.9 all-reduce.7
  1022.6 114.8 all-reduce.9
  1141.2 99.7 all-reduce.11
  1435.0 96.1 all-reduce.5
  1533.4 111.9 all-reduce.7
  1654.8 114.8 all-reduce.9
  1773.2 99.7 all-reduce.11
where the time goes:
time: 1940 us; the launch traced here: 1930 us
  waiting for transfers between devices  1210 us (62%)
  other arithmetic  407 us (21%)
  local copies, waits for them, and re-layouts  174 us (9%)
  matrix products  108 us (6%)
  loops' own time  22.1 us (1%)
    psum x12, waiting for transfers between devices, broadcast(): return lax.psum(block, axis)  1210 us
    another operation x42, other arithmetic, factor_share(): lower_factor = jnp.linalg.cholesky(safe_block)  237 us
    another operation x9, other arithmetic, factor_share(): jax.scipy.linalg.solve_triangular(lower_factor, identity, lower=True)  121 us
    dot_general x9, matrix products, product(): jnp.dot(first, second, precision=precise, preferred_element_type=jnp.floa...  71.4 us
  transfers between devices with their start and end apart: 12, of which 12 were waited for; matrix products, arithmetic and copies ran while one was open for 4% of the time, Pallas kernels for 0%

commit v1 on v0

v1 whole, which is shorter than its diff:
```python
import functools

import jax
import jax.numpy as jnp
from jax import lax
from jax.experimental import pallas as pl
from jax.experimental.pallas import tpu as pltpu
from jax.sharding import PartitionSpec as P

PANELS = 3
BS = 512
PAIRS = ((0, 0), (1, 0), (1, 1), (2, 0), (2, 1), (2, 2))
MESH = pl.DeviceIdType.MESH


def remote(src, dst, sems, index, row, col):
    return pltpu.make_async_remote_copy(
        src_ref=src,
        dst_ref=dst,
        send_sem=sems[0].at[index],
        recv_sem=sems[1].at[index],
        device_id=(row, col),
        device_id_type=MESH,
    )


class Plane:
    def __init__(self, cand, out, out_base, first, first_sum, second, sems, base, rows, place):
        self.cand, self.out, self.out_base = cand, out, out_base
        self.first, self.first_sum, self.second = first, first_sum, second
        self.sems, self.base, self.rows = sems, base, rows
        self.row, self.x, self.y = place
        self.copies = {}

    def peers(self, half, step):
        along_x = (half == 0) == (step == 0)
        for d in (1, 2, 3):
            if along_x:
                px, py = lax.rem(self.x + d, 4), self.y
                to = px
            else:
                px, py = self.x, lax.rem(self.y + d, 4)
                to = py
            yield d, to, px * 4 + py

    def mine(self, half):
        return (self.x, self.y) if half == 0 else (self.y, self.x)

    def start(self, phase):
        big, small = self.rows // 8, self.rows // 32
        for half in (0, 1):
            top = half * (self.rows // 2)
            a, b = self.mine(half)
            copies = []
            step = 0 if phase in (0, 3) else 1
            for d, to, col in self.peers(half, step):
                index = self.base + (phase * 2 + half) * 3 + d - 1
                if phase == 0:
                    src = self.cand.at[pl.ds(pl.multiple_of(top + to * big, 8), big), :]
                    dst = self.first.at[half, d - 1]
                elif phase == 1:
                    src = self.first_sum.at[half, pl.ds(pl.multiple_of(to * small, 8), small), :]
                    dst = self.second.at[half, d - 1]
                elif phase == 2:
                    at = pl.multiple_of(self.out_base + top + a * big + b * small, 8)
                    src = dst = self.out.at[pl.ds(at, small), :]
                else:
                    at = pl.multiple_of(self.out_base + top + a * big, 8)
                    src = dst = self.out.at[pl.ds(at, big), :]
                copy = remote(src, dst, self.sems, index, self.row, col)
                copy.start()
                copies.append(copy)
            self.copies[phase, half] = copies

    def finish(self, phase):
        big, small = self.rows // 8, self.rows // 32
        for half in (0, 1):
            for copy in self.copies[phase, half]:
                copy.wait_recv()
            top = half * (self.rows // 2)
            a, b = self.mine(half)
            if phase == 0:
                own = self.cand[pl.ds(pl.multiple_of(top + a * big, 8), big), :]
                self.first_sum[half] = (
                    own + self.first[half, 0] + self.first[half, 1] + self.first[half, 2]
                )
            elif phase == 1:
                own = self.first_sum[half, pl.ds(pl.multiple_of(b * small, 8), small), :]
                at = pl.multiple_of(self.out_base + top + a * big + b * small, 8)
                self.out[pl.ds(at, small), :] = (
                    own + self.second[half, 0] + self.second[half, 1] + self.second[half, 2]
                )

    def drain(self):
        for copies in self.copies.values():
            for copy in copies:
                copy.wait_send()


def share_kernel(flag_ref, m, p_out, q_out, d_out,
                 p_cand, q_cand, p_first, p_sum, p_second,
                 d_cand, d_first, d_sum, d_second, sib, ring, send_sem, recv_sem):
    row, col = lax.axis_index("row"), lax.axis_index("col")
    z, core = row // 2, lax.rem(row, 2)
    x, y = col // 4, lax.rem(col, 4)
    sems = (send_sem, recv_sem)
    sibling = z * 2 + (1 - core)
    up = lax.rem(z + 1, 8) * 2 + core
    down = lax.rem(z + 7, 8) * 2 + core

    barrier = pltpu.get_barrier_semaphore()
    places = [(sibling, col), (up, col), (down, col)]
    for d in (1, 2, 3):
        places.append((row, lax.rem(x + d, 4) * 4 + y))
        places.append((row, x * 4 + lax.rem(y + d, 4)))
    for place in places:
        pl.semaphore_signal(barrier, inc=1, device_id=place, device_id_type=MESH)

    for t in range(PANELS):
        p0, p1 = flag_ref[t * 2], flag_ref[t * 2 + 1]
        q0, q1 = flag_ref[6 + t * 2], flag_ref[6 + t * 2 + 1]

        def build(i, _, t=t, p0=p0, p1=p1, q0=q0, q1=q1):
            at = pl.multiple_of(i * 64, 64)
            p_cand[pl.ds(t * 1024 + at, 64), :] = (
                m[pl.ds(at, 64), :BS] * p0 + m[pl.ds(at, 64), BS:] * p1
            )
            return 0

        lax.fori_loop(0, 16, build, 0)

        def build_row(i, _, t=t, p0=p0, p1=p1, q0=q0, q1=q1):
            at = pl.multiple_of(i * 64, 64)
            both = m[pl.ds(at, 64), :] * q0 + m[pl.ds(512 + at, 64), :] * q1
            q_cand[pl.ds(t * 1024 + at, 64), :] = both[:, :BS]
            q_cand[pl.ds(t * 1024 + 512 + at, 64), :] = both[:, BS:]
            return 0

        lax.fori_loop(0, 8, build_row, 0)

    pl.semaphore_wait(barrier, 9)

    plane = Plane(p_cand, p_out, 0, p_first, p_sum, p_second, sems, 0, 3072, (row, x, y))
    plane.start(0)

    half_rows = 1536
    mine = pl.multiple_of(core * half_rows, 8)
    other = pl.multiple_of((1 - core) * half_rows, 8)
    swap = remote(q_cand.at[pl.ds(other, half_rows), :], sib, sems, 48, sibling, col)
    swap.start()
    swap.wait_recv()

    def merge(i, _):
        at = pl.multiple_of(i * 64, 64)
        sib[pl.ds(at, 64), :] = sib[pl.ds(at, 64), :] + q_cand[pl.ds(mine + at, 64), :]
        return 0

    lax.fori_loop(0, 24, merge, 0)

    def part(number, way):
        return pl.ds(pl.multiple_of(number * 192 + way * 96, 8), 96)

    pending = []
    for step in range(7):
        copies = []
        for way in (0, 1):
            number = lax.rem(z + 7 - step, 8) if way == 0 else lax.rem(z + 1 + step, 8)
            copy = remote(sib.at[part(number, way), :], ring.at[way, step], sems,
                          50 + step * 2 + way, up if way == 0 else down, col)
            copy.start()
            copies.append(copy)
        for way in (0, 1):
            copies[way].wait_recv()
            number = lax.rem(z + 6 - step + 8, 8) if way == 0 else lax.rem(z + 2 + step, 8)
            if step < 6:
                sib[part(number, way), :] = sib[part(number, way), :] + ring[way, step]
            else:
                at = pl.multiple_of(mine + z * 192 + way * 96, 8)
                q_out[pl.ds(at, 96), :] = sib[part(number, way), :] + ring[way, step]
        pending += copies
        if step == 5:
            plane.finish(0)
            plane.start(1)
    plane.finish(1)
    plane.start(2)
    for step in range(7):
        copies = []
        for way in (0, 1):
            number = lax.rem(z + 8 - step, 8) if way == 0 else lax.rem(z + step, 8)
            at = pl.multiple_of(mine + number * 192 + way * 96, 8)
            copy = remote(q_out.at[pl.ds(at, 96), :], q_out.at[pl.ds(at, 96), :], sems,
                          64 + step * 2 + way, up if way == 0 else down, col)
            copy.start()
            copies.append(copy)
        if step == 1:
            plane.finish(2)
            plane.start(3)
        for way in (0, 1):
            copies[way].wait_recv()
        pending += copies
    final = remote(q_out.at[pl.ds(mine, half_rows), :], q_out.at[pl.ds(mine, half_rows), :],
                   sems, 49, sibling, col)
    final.start()
    final.wait_recv()

    for b, (t, s) in enumerate(PAIRS):
        w0, w1 = flag_ref[s * 2], flag_ref[s * 2 + 1]

        def pick(i, _, t=t, b=b, w0=w0, w1=w1):
            at = pl.multiple_of(i * 64, 64)
            src = pl.multiple_of(t * 1024 + core * 256 + at, 8)
            d_cand[pl.ds(b * 256 + at, 64), :] = (
                q_out[pl.ds(src, 64), :] * w0 + q_out[pl.ds(src + 512, 64), :] * w1
            )
            return 0

        lax.fori_loop(0, 4, pick, 0)
    cross = Plane(d_cand, d_out, mine, d_first, d_sum, d_second, sems, 24, 1536, (row, x, y))
    plane.finish(3)
    for phase in range(4):
        cross.start(phase)
        cross.finish(phase)
    last = remote(d_out.at[pl.ds(mine, half_rows), :], d_out.at[pl.ds(mine, half_rows), :],
                  sems, 78, sibling, col)
    last.start()
    last.wait_recv()
    for copy in pending + [swap, final, last]:
        copy.wait_send()
    plane.drain()
    cross.drain()


def share(m, flags):
    f32 = jnp.float32
    whole = jax.ShapeDtypeStruct((3072, BS), f32)
    vmem = pl.BlockSpec(memory_space=pltpu.VMEM)
    return pl.pallas_call(
        share_kernel,
        out_shape=(whole, whole, whole),
        in_specs=[pl.BlockSpec(memory_space=pltpu.SMEM), vmem],
        out_specs=(vmem, vmem, vmem),
        scratch_shapes=[
            pltpu.VMEM((3072, BS), f32),
            pltpu.VMEM((3072, BS), f32),
            pltpu.VMEM((2, 3, 384, BS), f32),
            pltpu.VMEM((2, 384, BS), f32),
            pltpu.VMEM((2, 3, 96, BS), f32),
            pltpu.VMEM((1536, BS), f32),
            pltpu.VMEM((2, 3, 192, BS), f32),
            pltpu.VMEM((2, 192, BS), f32),
            pltpu.VMEM((2, 3, 48, BS), f32),
            pltpu.VMEM((1536, BS), f32),
            pltpu.VMEM((2, 7, 96, BS), f32),
            pltpu.SemaphoreType.DMA((80,)),
            pltpu.SemaphoreType.DMA((80,)),
        ],
        compiler_params=pltpu.CompilerParams(
            collective_id=0, has_side_effects=True, vmem_limit_bytes=60 * 1024 * 1024
        ),
    )(flags, m)


def split(v):
    high = v.astype(jnp.bfloat16)
    low = (v - high.astype(jnp.float32)).astype(jnp.bfloat16)
    return high, low


def dot_first(a, b):
    return lax.dot_general(a, b, (((0,), (0,)), ((), ())), preferred_element_type=jnp.float32)


STRIP = 16


def invert_kernel(a_ref, u_ref, w_ref, m):
    m[:, :BS] = a_ref[...]
    rows = lax.broadcasted_iota(jnp.int32, (BS, BS), 0)
    cols = lax.broadcasted_iota(jnp.int32, (BS, BS), 1)
    m[:, BS:] = jnp.where(rows == cols, 1.0, 0.0)
    sub = lax.broadcasted_iota(jnp.int32, (STRIP, 128), 0)
    lane = lax.broadcasted_iota(jnp.int32, (STRIP, 128), 1)
    tile = (STRIP, 128)

    def outer(o, _):
        r0 = pl.multiple_of(o * 128, 128)
        for i in range(128 // STRIP):
            rr = r0 + i * STRIP
            strip = [m[pl.ds(rr, STRIP), pl.ds(k * 128, 128)] for k in range(8)]
            diag = m[pl.ds(rr, STRIP), pl.ds(r0, 128)]
            column = [
                jnp.broadcast_to(diag[:, i * STRIP + j : i * STRIP + j + 1], tile)
                for j in range(STRIP)
            ]
            for j in range(STRIP):
                scale = lax.rsqrt(jnp.broadcast_to(column[j][j : j + 1, :], tile))
                solved = column[j] * scale
                below = jnp.where(sub > j, solved, 0.0)
                for k in range(j + 1, STRIP):
                    column[k] = column[k] - below * jnp.broadcast_to(solved[k : k + 1, :], tile)
                for k in range(8):
                    row = jnp.broadcast_to(strip[k][j : j + 1, :], tile) * scale
                    strip[k] = jnp.where(sub == j, row, strip[k] - below * row)
            for k in range(4):
                strip[k] = jnp.where(lane + k * 128 >= sub + rr, strip[k], 0.0)
            for k in range(8):
                m[pl.ds(rr, STRIP), pl.ds(k * 128, 128)] = strip[k]
            if i < 128 // STRIP - 1:
                rest = 128 - (i + 1) * STRIP
                ph, plow = split(jnp.concatenate(strip, axis=1))
                dh, dl = split(m[pl.ds(rr, STRIP), pl.ds(r0, 128)])
                left = jnp.concatenate([dh, dh, dl], axis=0)
                right = jnp.concatenate([ph, plow, ph], axis=0)
                change = dot_first(left, right)
                below_rows = pl.ds(rr + STRIP, rest)
                m[below_rows, :] = m[below_rows, :] - change[(i + 1) * STRIP :, :]
        ph, plow = split(m[pl.ds(r0, 128), :])
        for k in range(4):

            @pl.when(k > o)
            def _():
                lh, ll = ph[:, k * 128 : (k + 1) * 128], plow[:, k * 128 : (k + 1) * 128]
                left = jnp.concatenate([lh, lh, ll], axis=0)
                right = jnp.concatenate([ph, plow, ph], axis=0)
                at = pl.ds(k * 128, 128)
                m[at, :] = m[at, :] - dot_first(left, right)

        return 0

    lax.fori_loop(0, 4, outer, 0)
    u_ref[...] = m[:, :BS]
    w_ref[...] = m[:, BS:]


def invert(a):
    vmem = pl.BlockSpec(memory_space=pltpu.VMEM)
    return pl.pallas_call(
        invert_kernel,
        out_shape=(jax.ShapeDtypeStruct((BS, BS), jnp.float32),) * 2,
        in_specs=[vmem],
        out_specs=(vmem, vmem),
        scratch_shapes=[pltpu.VMEM((BS, 2 * BS), jnp.float32)],
        compiler_params=pltpu.CompilerParams(vmem_limit_bytes=32 * 1024 * 1024),
    )(a)


def product(first, second):
    return jnp.dot(first, second, precision=lax.Precision.HIGH, preferred_element_type=jnp.float32)


def per_device(front_values, block_pattern, panel_order):
    row, col = lax.axis_index("row"), lax.axis_index("col")
    pattern = lax.dynamic_slice(
        block_pattern.reshape(2, 16, 2, 16), (0, row, 0, col), (2, 1, 2, 1)
    ).reshape(2, 2).astype(jnp.float32)
    m = (front_values.reshape(2, BS, 2, BS) * pattern[:, None, :, None]).reshape(2 * BS, 2 * BS)
    pivots = panel_order[:PANELS]
    slots = jnp.arange(2, dtype=jnp.int32)
    here_col = (pivots[:, None] == slots[None, :] * 16 + col).astype(jnp.float32).reshape(6)
    here_row = (pivots[:, None] == slots[None, :] * 16 + row).astype(jnp.float32).reshape(6)
    p_all, q_all, d_all = share(m, jnp.concatenate([here_col, here_row]))
    p_all = p_all.reshape(PANELS, 2 * BS, BS)
    q_all = q_all.reshape(PANELS, 2, BS, BS).transpose(0, 2, 1, 3).reshape(PANELS, BS, 2 * BS)
    d_all = d_all.reshape(2, 6, BS // 2, BS).transpose(1, 0, 2, 3).reshape(6, BS, BS)
    d = {pair: d_all[i] for i, pair in enumerate(PAIRS)}
    crossing = {}
    lowers, lefts, rights = [], [], []
    for t in range(PANELS):
        upper, inverse = invert(d[t, t])
        lowers.append(upper.T)
        for s in range(t + 1, PANELS):
            crossing[t, s] = product(inverse, d[s, t].T)
        for a in range(t + 1, PANELS):
            for b in range(t + 1, a + 1):
                d[a, b] = d[a, b] - product(crossing[t, a].T, crossing[t, b])
        left, right = p_all[t], q_all[t]
        for s in range(t):
            left = left - product(lefts[s], crossing[s, t])
            right = right - product(crossing[s, t].T, rights[s])
        lefts.append(product(left, inverse.T))
        rights.append(product(inverse, right))
    updated = m
    row_ids = slots * 16 + row
    col_ids = slots * 16 + col
    row_turn = jnp.where(row_ids[:, None] == pivots[None, :], 0, 3)
    row_turn = jnp.min(row_turn + jnp.arange(3)[None, :] * (row_turn == 0), axis=1)
    col_turn = jnp.where(col_ids[:, None] == pivots[None, :], 0, 3)
    col_turn = jnp.min(col_turn + jnp.arange(3)[None, :] * (col_turn == 0), axis=1)
    updated = m - product(jnp.concatenate(lefts, axis=1), jnp.concatenate(rights, axis=0))
    blocks = []
    for a in range(2):
        line = []
        for b in range(2):
            block = updated[a * BS : (a + 1) * BS, b * BS : (b + 1) * BS]
            for t in range(PANELS):
                left = lefts[t][a * BS : (a + 1) * BS]
                right = rights[t][:, b * BS : (b + 1) * BS]
                block = jnp.where((col_turn[b] == t) & (row_turn[a] > t), left, block)
                block = jnp.where((row_turn[a] == t) & (col_turn[b] > t), right, block)
                block = jnp.where((row_turn[a] == t) & (col_turn[b] == t), lowers[t], block)
            line.append(block)
        blocks.append(jnp.concatenate(line, axis=1))
    return jnp.concatenate(blocks, axis=0).reshape(front_values.shape)


def solution(mesh):
    return jax.shard_map(
        per_device,
        mesh=mesh,
        in_specs=(P(None, "row", None, None, "col", None), P(), P()),
        out_specs=P(None, "row", None, None, "col", None),
        check_vma=False,
    )
```

time: 1940 us -> 442 us (0.23)
  waiting for transfers between devices: 1210 us -> 0 us
  other arithmetic: 407 us -> 41.9 us
  Pallas kernels: 0 us -> 238 us
  local copies, waits for them, and re-layouts: 174 us -> 92.7 us
  matrix products: 108 us -> 49.2 us
  loops' own time: 22.1 us -> 0 us
    psum x12 -> x0, waiting for transfers between devices: 1210 us -> none  [broadcast(): return lax.psum(block, axis)]
    another operation x51 -> x0, other arithmetic: 358 us -> none  [the longest x42 237 us: factor_share(): lower_factor = jnp.linalg.cholesky(safe_block)]
    pallas_call x0 -> x4, Pallas kernels: none -> 238 us  [the longest x1 177 us: share(): pl.pallas_call(share_kernel, out_shape=(whole, whole, whole), in_specs=[p...]
    another operation x111 -> x0, local copies, waits for them, and re-layouts: 38.6 us -> none
    dynamic_slice x25 -> x1, local copies, waits for them, and re-layouts: 37.9 us -> 0.08 us  [per_device(): lax.dynamic_slice(block_pattern.reshape(2, 16, 2, 16), (0, row, 0, col),...]
    while x66 -> x0, local copies, waits for them, and re-layouts: 36.6 us -> none
    another operation x39 -> x0, matrix products: 36.5 us -> none  [the longest x21 24.3 us: factor_share(): jax.scipy.linalg.solve_triangular(lower_factor, identity, lower=True)]
    unnamed x3 -> x65, local copies, waits for them, and re-layouts: 0.11 us -> 26.9 us
  transfers between devices with their start and end apart: 12 -> 0, of which waited for: 12 -> 0; matrix products, arithmetic and copies ran while one was open for 4% -> 0% of each run, Pallas kernels for 0% -> 0%
where the time goes in v1:
time: 442 us; the launch traced here: 437 us
  Pallas kernels  238 us (54%)
  local copies, waits for them, and re-layouts  92.7 us (21%)
  matrix products  49.2 us (11%)
  other arithmetic  41.9 us (9%)
  between operations  15.9 us (4%)
    pallas_call x1, Pallas kernels, share(): pl.pallas_call(share_kernel, out_shape=(whole, whole, whole), in_specs=[p...  177 us
    pallas_call x3, Pallas kernels, invert(): pl.pallas_call(invert_kernel, out_shape=(jax.ShapeDtypeStruct((BS, BS), j...  60.8 us
    dot_general x20, matrix products, product(): jnp.dot(first, second, precision=lax.Precision.HIGH, preferred_element_ty...  49.2 us
    unnamed x65, local copies, waits for them, and re-layouts  26.9 us
    reshape x2, local copies, waits for them, and re-layouts, per_device(): return jnp.concatenate(blocks, axis=0).reshape(front_values.shape)  17.4 us
    unnamed x3, other arithmetic  15.8 us
    select_n x4, other arithmetic, per_device(): block = jnp.where((row_turn[a] == t) & (col_turn[b] == t), lowers[t], block)  14.7 us

profile of v1, /device:TPU:1, one launch (start us, length us, event | category | flops | bytes accessed | tf_op | source)
XLA Modules:
  0.0 437.4 jit_solution(13268382033611179007)
XLA Ops:
  19.3 1.1 mul.58
  20.5 3.0 copy.53
  23.4 15.8 %reduce = f32[2,512,2,512]{3,2,1,0:T(2,128)} reduce(f32[2,1,512,2,1,512]{5,4,3,2,1,0:T(1,128)} %param.3, f32[]{:T(128)} %constant.50), dimensions={1,4}, to_apply=%param.3.reduce_sub_computation | reduce | bytes 8388612 | tf_op args[0]
  39.3 5.2 %copy.52 = f32[128,8,2,512]{3,1,2,0:T(8,128)} copy(f32[128,8,2,512]{3,2,1,0:T(2,128)} %bitcast.119) | data formatting | bytes 8388608
  44.5 5.3 %copy.44 = f32[1024,1024]{0,1:T(8,128)} copy(f32[1024,1024]{1,0:T(8,128)} %bitcast.120) | data formatting | bytes 8388608 | tf_op jit(solution)/shard_map/reshape | solution.py:356
  49.8 6.8 %mul.60 = f32[1024,1024]{0,1:T(8,128)} multiply(f32[1024,1024]{0,1:T(8,128)} %copy.44, f32[1024,1024]{0,1:T(8,128)} %bitcast.117) | non-fusion elementwise | flops 1048576 | bytes 12582912 | tf_op jit(solution)/shard_map/mul | solution.py:356
  56.7 5.4 %copy.32.m = f32[1024,1024]{1,0:T(8,128)} copy(f32[1024,1024]{0,1:T(8,128)} %mul.60) | data formatting | bytes 8388608 | tf_op jit(solution)/shard_map/mul | solution.py:356
  62.0 176.9 %shard_map.37 = (f32[3072,512]{1,0:T(8,128)}, f32[3072,512]{1,0:T(8,128)}, f32[3072,512]{1,0:T(8,128)}) custom-call(f32[12]{0:T(128)} %add_convert_fusion.flag_ref, f32[1024,1024]{1,0:T(8,128)} %copy.32.m), custom_call_target="tpu_custom_call" | custom-call | tf_op jit(solution)/shard_map/pallas_call | solution.py:237
  239.0 6.1 %copy.55 = f32[2,6,256,512]{3,2,0,1:T(8,128)} copy(f32[2,6,256,512]{3,2,1,0:T(8,128)} %bitcast.125) | data formatting | bytes 12582912 | tf_op jit(solution)/shard_map/reshape | solution.py:364
  245.1 6.7 %copy.34 = f32[3,2,512,512]{2,3,1,0:T(8,128)} copy(f32[3,2,512,512]{3,2,1,0:T(8,128)} %bitcast.124) | data formatting | bytes 12582912 | tf_op jit(solution)/shard_map/reshape | solution.py:363
  251.8 5.5 %fusion.70 = (f32[1,2,256,512]{3,2,1,0:T(8,128)}, f32[1,2,256,512]{3,2,1,0:T(8,128)}, f32[1,2,256,512]{3,2,1,0:T(8,128)}, f32[1,2,256,512]{3,2,1,0:T(8,128)S(1)}...) fusion(f32[6,2,256,512]{3,2,1,0:T(8,128)} %bitcast.116), kind=kLoop, calls=%fused_computation.86 | loop fusion | bytes 12582912 | tf_op jit(solution)/shard_map/slice | solution.py:365
  257.6 2.7 fusion.69
  260.3 3.0 copy.35
  263.3 2.9 copy.36
  266.3 20.2 %shard_map.38 = (f32[512,512]{1,0:T(8,128)S(1)}, f32[512,512]{1,0:T(8,128)S(1)}) custom-call(f32[512,512]{1,0:T(8,128)S(1)} %bitcast.112), custom_call_target="tpu_custom_call" | custom-call | tf_op jit(solution)/shard_map/pallas_call | solution.py:337
  286.5 3.5 fusion.79
  290.0 1.0 fusion.77
  295.8 1.8 fusion.17
  297.6 20.2 %shard_map.39 = (f32[512,512]{1,0:T(8,128)S(1)}, f32[512,512]{1,0:T(8,128)S(1)}) custom-call(f32[512,512]{1,0:T(8,128)S(1)} %convolution_subtract_fusion.2.a_ref), custom_call_target="tpu_custom_call" | custom-call | tf_op jit(solution)/shard_map/pallas_call | solution.py:337
  318.9 1.0 convolution_subtract_fusion.a_ref
  320.0 20.4 %shard_map.40 = (f32[512,512]{1,0:T(8,128)S(1)}, f32[512,512]{1,0:T(8,128)S(1)}) custom-call(f32[512,512]{1,0:T(8,128)S(1)} %convolution_subtract_fusion.a_ref), custom_call_target="tpu_custom_call" | custom-call | tf_op jit(solution)/shard_map/pallas_call | solution.py:337
  340.4 1.8 fusion.84
  342.2 1.9 fusion.13
  344.2 1.9 fusion.81
  346.5 1.9 fusion.22
  348.4 2.0 fusion.82
  350.4 1.9 fusion.85
  352.3 2.0 fusion.83
  354.3 3.3 fusion.11
  357.6 1.9 fusion.80
  359.6 3.3 fusion.20
  362.9 14.7 %fusion.25 = f32[1024,1024]{0,1:T(8,128)} fusion(f32[1024,1024]{0,1:T(8,128)} %mul.60, f32[512,1024]{1,0:T(8,128)} %fusion.20, f32[512,1024]{1,0:T(8,128)} %copy-done.7, f32[512,1024]{1,0:T(8,128)S(1)} %fusion.79, f32[1024,512]{0,1:T(8,128)} %fusion.11, f32[1024,512]{0,1:T(8,128)S(1)} %copy-done.4, f32[1024,512]{0,1:T(8,128)S(1)} %fusion.17), kind=kOutput, calls=%fused_computation.31 | convolution fusion | flops 9671016448 | bytes 20971520 | tf_op jit(solution)/shard_map/dot_general | solution.py:348
  377.6 1.6 fusion.71
  379.2 2.6 copy.48
  381.7 3.0 fusion.72
  384.8 2.6 copy.47
  387.3 3.1 fusion.73
  390.4 2.6 copy.46
  393.1 4.7 %fusion.45 = f32[512,512]{0,1:T(8,128)} fusion(f32[512,512]{0,1:T(8,128)} %copy.46, f32[512,512]{0,1:T(8,128)} %copy.47, f32[512,512]{0,1:T(8,128)} %copy.48, f32[1024,1024]{0,1:T(8,128)} %fusion.25, f32[512,512]{1,0:T(8,128)S(1)} %get-tuple-element.22, f32[512,512]{1,0:T(8,128)S(1)} %get-tuple-element.21, f32[512,512]{1,0:T(8,128)S(1)} %get-tuple-element.17, ...), kind=kLoop, calls=%fused_computation.49 | loop fusion | flops 2359296 | bytes 11534345 | tf_op jit(solution)/shard_map/jit(_where)/select_n | solution.py:400
  398.4 3.6 fusion.61
  402.0 2.6 copy.49
  404.6 2.6 copy.50
  407.2 2.6 copy.51
  409.8 3.7 fusion.37
  414.7 2.7 fusion.53
  417.4 2.3 maximum_maximum_fusion
  419.7 6.6 %reshape.166 = f32[2,1,512,2,1,512]{2,0,5,3,4,1:T(2,128)} reshape(f32[1024,1024]{0,1:T(8,128)} %maximum_maximum_fusion) | data formatting | bytes 8388608 | tf_op jit(solution)/shard_map/reshape | solution.py:403
  426.3 10.9 %copy.43 = f32[2,1,512,2,1,512]{5,4,3,2,1,0:T(1,128)} copy(f32[2,1,512,2,1,512]{2,0,5,3,4,1:T(2,128)} %reshape.166) | data formatting | bytes 8388608 | tf_op jit(solution)/shard_map/reshape | solution.py:403
  (76 shorter events, 12.4 us)
Async XLA Ops:
  251.8 5.5 %slice-start = ((s8[6291456]{0:T(1024)(128)(4,1)}), s8[4194304]{0:T(1024)(128)(4,1)S(1)}, s32[]{:S(2)}) async-start(s8[6291456]{0:T(1024)(128)(4,1)} %bitcast.113), calls=%async_computation | async-start | bytes 8388608
  251.8 5.8 %slice-start.1 = ((s8[6291456]{0:T(1024)(128)(4,1)}), s8[2097152]{0:T(1024)(128)(4,1)S(1)}, s32[]{:S(2)}) async-start(s8[6291456]{0:T(1024)(128)(4,1)} %bitcast.113), calls=%async_computation.1 | async-start | bytes 4194304
  286.4 3.5 copy-start.18
  291.0 1.2 copy-start.21
  291.0 2.2 copy-start.20
  292.3 3.5 slice-start.2
  293.3 1.4 copy-start.19
  293.3 2.5 slice-start.3
  297.6 65.3 %copy-start = (f32[1024,512]{0,1:T(8,128)}, f32[1024,512]{0,1:T(8,128)S(1)}, u32[]{:S(2)}) copy-start(f32[1024,512]{0,1:T(8,128)S(1)} %fusion.17) | copy-start | bytes 6291460
  344.1 6.3 %copy-start.3 = (f32[1024,512]{0,1:T(8,128)}, f32[1024,512]{0,1:T(8,128)S(1)}, u32[]{:S(2)}) copy-start(f32[1024,512]{0,1:T(8,128)S(1)} %fusion.13) | copy-start | bytes 6291460
  344.1 2.3 copy-start.16
  348.4 2.0 copy-start.7
  357.6 1.9 copy-start.17
  359.6 3.3 copy-start.4
  393.1 4.7 %copy-start.1 = (f32[1024,512]{0,1:T(8,128)S(1)}, f32[1024,512]{0,1:T(8,128)}, u32[]{:S(2)}) copy-start(f32[1024,512]{0,1:T(8,128)} %copy-done) | copy-start | bytes 6291460
  393.1 4.7 %copy-start.5 = (f32[1024,512]{0,1:T(8,128)S(1)}, f32[1024,512]{0,1:T(8,128)}, u32[]{:S(2)}) copy-start(f32[1024,512]{0,1:T(8,128)} %copy-done.3) | copy-start | bytes 6291460
  393.1 4.7 %copy-start.8 = (f32[1024,512]{0,1:T(8,128)S(1)}, f32[1024,512]{0,1:T(8,128)}, u32[]{:S(2)}) copy-start(f32[1024,512]{0,1:T(8,128)} %fusion.11) | copy-start | bytes 6291460
  393.1 4.7 %copy-start.10 = (f32[512,512]{0,1:T(8,128)S(1)}, f32[512,512]{0,1:T(8,128)}, u32[]{:S(2)}) copy-start(f32[512,512]{0,1:T(8,128)} %copy.48) | copy-start | bytes 3145732
  393.1 4.7 %copy-start.14 = (f32[512,512]{0,1:T(8,128)S(1)}, f32[512,512]{0,1:T(8,128)}, u32[]{:S(2)}) copy-start(f32[512,512]{0,1:T(8,128)} %copy.47) | copy-start | bytes 3145732
  393.1 5.3 %copy-start.15 = (f32[512,512]{0,1:T(8,128)S(1)}, f32[512,512]{0,1:T(8,128)}, u32[]{:S(2)}) copy-start(f32[512,512]{0,1:T(8,128)} %copy.46) | copy-start | bytes 3145732
  409.7 3.8 copy-start.2
  409.7 3.8 copy-start.6
  409.7 4.1 copy-start.9
  409.7 4.3 copy-start.11
  409.7 4.6 %copy-start.12 = (f32[512,512]{0,1:T(8,128)S(1)}, f32[512,512]{0,1:T(8,128)}, u32[]{:S(2)}) copy-start(f32[512,512]{0,1:T(8,128)} %copy.50) | copy-start | bytes 3145732
  409.7 4.9 %copy-start.13 = (f32[512,512]{0,1:T(8,128)S(1)}, f32[512,512]{0,1:T(8,128)}, u32[]{:S(2)}) copy-start(f32[512,512]{0,1:T(8,128)} %copy.51) | copy-start | bytes 3145732
  414.7 2.7 copy-start.22
  414.7 2.7 copy-start.23
